TPU v7x, 128 devices: a whole 4x4x4 slice. The times are simulated.
128 devices in a mesh: grp: 2 (over y_hi), tp: 32 (over y_lo, x, z), rep: 2 (over core).
Axes of the slice: x: 4, y: 4 (y_hi: 2, y_lo: 2; y = y_hi * 2 + y_lo), z: 4, core: 2. Of those that a mesh axis runs over, the one named last changes fastest.
Arguments:
- hidden_states: bfloat16 [8, 8192], replicated, may hold values from -24 to 24
- attn_gain: float32 [8192], replicated, may hold values from 0.1 to 1.9
- ffn_gain: float32 [8192], replicated, may hold values from 0.1 to 1.9
- w_query: bfloat16 [8192, 2, 32, 128], P('grp', 'rep', 'tp'), may hold values from -0.0625 to 0.0625
- w_keyval: bfloat16 [8192, 2, 1024], P('grp', 'rep', 'tp'), may hold values from -0.0625 to 0.0625
- w_out: bfloat16 [2, 32, 128, 8192], P('rep', 'tp', None, 'grp'), may hold values from -0.0625 to 0.0625
- w_gate: bfloat16 [8192, 14336], P('grp', ('tp', 'rep')), may hold values from -0.0625 to 0.0625
- w_up: bfloat16 [8192, 14336], P('grp', ('tp', 'rep')), may hold values from -0.0625 to 0.0625
- w_down: bfloat16 [14336, 8192], P(('tp', 'rep'), 'grp'), may hold values from -0.125 to 0.125
- kv_cache: bfloat16 [8, 32768, 8, 256], P(None, ('grp', 'tp'), 'rep'), may hold values from -70 to 70
- lengths: int32 [8], replicated, may hold values from 1 to 32768, as said below
- first_shard: int32 [8], replicated, may hold values from 0 to 63
Outputs:
- layer_out: bfloat16 [8, 8192], P(None, ('grp', 'tp', 'rep'))
Inputs may be any that keep to these rules, and one draw needn't show every extreme that they name: `lengths`: some request has exactly 32768 cached tokens in every draw.
All inputs are finite; a program needn't handle non-finite values.
Results may differ from a plain program's by a relative error of at most 0.025.
Values may be sent and summed in bfloat16 or wider, within the bound.
A program may use at most 128 MiB of HBM per device.

v0:
```python
import jax
import jax.numpy as jnp
from jax import lax
from jax.sharding import PartitionSpec as P

epsilon = 1e-05
base_freq = 500000.0
masked = -1e30


def joined(shard, axis, combine):
    everything = jax.tree.map(
        lambda part, kind: lax.all_gather(part.astype(kind), axis),
        shard,
        jax.tree.map(lambda a: jnp.bfloat16 if a.dtype == jnp.float32 else a.dtype, shard),
    )

    def take(k):
        return jax.tree.map(lambda part, own: part[k].astype(own.dtype), everything, shard)

    return lax.fori_loop(
        1, lax.axis_size(axis), lambda k, so_far: combine(so_far, take(k)), take(0)
    )


def scaled_norm(values_in, gain):
    return (
        values_in
        * lax.rsqrt(jnp.mean(values_in * values_in, axis=-1, keepdims=True) + epsilon)
        * gain
    )


def rotary(pairs_in, positions):
    head_width = pairs_in.shape[-1]
    frequency = base_freq ** (-(2.0 * jnp.arange(head_width // 2, dtype=jnp.float32)) / head_width)
    angles = positions.astype(jnp.float32)[:, None] * frequency[None, :]
    cos_part = jnp.cos(angles)[:, None, :]
    sin_part = jnp.sin(angles)[:, None, :]
    halves = pairs_in.reshape(pairs_in.shape[:-1] + (head_width // 2, 2))
    real_part = halves[..., 0]
    imag_part = halves[..., 1]
    turned = jnp.stack(
        (real_part * cos_part - imag_part * sin_part, real_part * sin_part + imag_part * cos_part),
        axis=-1,
    )
    return turned.reshape(pairs_in.shape)


def column_sum(proj_term):
    return lax.psum_scatter(proj_term, ("tp", "rep"), scatter_dimension=1, tiled=True)


def combine_parts(left_part, right_part):
    left_peak, left_sum, left_num = left_part
    right_peak, right_sum, right_num = right_part
    joint_peak = jnp.maximum(left_peak, right_peak)
    left_scale = jnp.exp(left_peak - joint_peak)
    right_scale = jnp.exp(right_peak - joint_peak)
    return (
        joint_peak,
        left_sum * left_scale + right_sum * right_scale,
        left_num * left_scale[..., None] + right_num * right_scale[..., None],
    )


def on_device(
    hidden_states,
    attn_gain,
    ffn_gain,
    w_query,
    w_keyval,
    w_out,
    w_gate,
    w_up,
    w_down,
    kv_cache,
    lengths,
    first_shard,
):
    group_side = lax.axis_index("grp")
    shard_index = lax.axis_index("tp")
    copy_index = lax.axis_index("rep")
    shard_count = lax.axis_size("tp")
    copy_count = lax.axis_size("rep")
    group_count = lax.axis_size("grp")
    requests, model_width = hidden_states.shape
    row_width = w_query.shape[0]
    heads_dev = w_query.shape[2]
    head_dim = w_query.shape[3]
    kv_local = kv_cache.shape[2]
    ctx_dev = kv_cache.shape[1]
    half_heads = heads_dev * shard_count
    group_size = half_heads // kv_local
    inv_scale = head_dim ** (-0.5)
    states = hidden_states.astype(jnp.float32)
    normed = scaled_norm(states, attn_gain).astype(jnp.bfloat16)
    normed_half = lax.dynamic_slice_in_dim(normed, group_side * row_width, row_width, 1)
    query_part = jnp.dot(
        normed_half,
        w_query.reshape(row_width, heads_dev * head_dim),
        preferred_element_type=jnp.float32,
    )
    keyval_part = jnp.dot(
        normed_half, w_keyval.reshape(row_width, -1), preferred_element_type=jnp.float32
    )
    query_sum, keyval_sum = lax.psum((query_part, keyval_part), "grp")
    outgoing = jnp.concatenate(
        (query_sum.astype(jnp.bfloat16), keyval_sum.astype(jnp.bfloat16)), axis=1
    )
    gathered = lax.all_gather(outgoing, "tp", axis=1, tiled=True).reshape(requests, shard_count, -1)
    query_all = gathered[:, :, : heads_dev * head_dim]
    keyval_new = gathered[:, :, heads_dev * head_dim :].reshape(requests, kv_local, 2 * head_dim)
    query_rot = rotary(query_all.astype(jnp.float32), lengths).astype(jnp.bfloat16)
    key_rot = rotary(keyval_new[:, :, :head_dim].astype(jnp.float32), lengths).astype(jnp.bfloat16)
    new_value = keyval_new[:, :, head_dim:]
    block_index = group_side * shard_count + shard_index
    block_total = group_count * shard_count
    position = ((block_index - first_shard) % block_total)[:, None] * ctx_dev + jnp.arange(
        ctx_dev, dtype=jnp.int32
    )[None, :]
    live_slot = position < lengths[:, None]
    q_group = query_rot.reshape(requests, kv_local, group_size, head_dim)
    cached_keys = kv_cache[..., :head_dim]
    cached_values = kv_cache[..., head_dim:]
    scores = (
        jnp.einsum("bgid,bcgd->bgic", q_group, cached_keys, preferred_element_type=jnp.float32)
        * inv_scale
    )
    scores = jnp.where(live_slot[:, None, None, :], scores, masked)
    local_peak = jnp.max(scores, axis=-1)
    weights = jnp.where(live_slot[:, None, None, :], jnp.exp(scores - local_peak[..., None]), 0.0)
    weight_sum = jnp.sum(weights, axis=-1)
    numerator = jnp.einsum(
        "bgic,bcgd->bgid",
        weights.astype(jnp.bfloat16),
        cached_values,
        preferred_element_type=jnp.float32,
    )
    partial_value = (
        local_peak.reshape(requests, half_heads),
        weight_sum.reshape(requests, half_heads),
        numerator.reshape(requests, half_heads, head_dim),
    )
    own_score = (
        jnp.sum(
            q_group.astype(jnp.float32) * key_rot.astype(jnp.float32)[:, :, None, :], axis=-1
        ).reshape(requests, half_heads)
        * inv_scale
    )
    value_heads = jnp.repeat(new_value, group_size, axis=1)
    head_start = shard_index * heads_dev
    peak_score, weight_sum, numerator = joined(partial_value, ("grp", "tp"), combine_parts)
    peak_score = lax.dynamic_slice_in_dim(peak_score, head_start, heads_dev, 1)
    weight_sum = lax.dynamic_slice_in_dim(weight_sum, head_start, heads_dev, 1)
    numerator = lax.dynamic_slice_in_dim(numerator, head_start, heads_dev, 1)
    own_score = lax.dynamic_slice_in_dim(own_score, head_start, heads_dev, 1)
    value_heads = lax.dynamic_slice_in_dim(value_heads, head_start, heads_dev, 1)
    final_peak = jnp.maximum(peak_score, own_score)
    keep_scale = jnp.exp(peak_score - final_peak)
    own_weight = jnp.exp(own_score - final_peak)
    denominator = weight_sum * keep_scale + own_weight
    own_rounded = lax.optimization_barrier(own_weight.astype(jnp.bfloat16)).astype(jnp.float32)
    numerator = numerator * keep_scale[..., None] + own_rounded[..., None] * value_heads.astype(
        jnp.float32
    )
    attended = (
        (numerator / denominator[..., None])
        .astype(jnp.bfloat16)
        .reshape(requests, heads_dev * head_dim)
    )
    proj_term = jnp.dot(
        attended, w_out.reshape(heads_dev * head_dim, -1), preferred_element_type=jnp.float32
    )
    half_width = proj_term.shape[1]
    block_width = half_width // (shard_count * copy_count)
    local_start = (shard_index * copy_count + copy_index) * block_width
    states_half = lax.dynamic_slice_in_dim(states, group_side * half_width, half_width, 1)
    proj_part = column_sum(proj_term)
    middle_part = (
        lax.dynamic_slice_in_dim(states_half, local_start, block_width, 1) + proj_part
    ).astype(jnp.bfloat16)
    middle = lax.all_gather(middle_part, ("grp", "tp", "rep"), axis=1, tiled=True)
    normed_ffn = scaled_norm(middle.astype(jnp.float32), ffn_gain).astype(jnp.bfloat16)
    ffn_half = lax.dynamic_slice_in_dim(normed_ffn, group_side * row_width, row_width, 1)
    gate_part = jnp.dot(ffn_half, w_gate, preferred_element_type=jnp.float32)
    up_part = jnp.dot(ffn_half, w_up, preferred_element_type=jnp.float32)
    gate_term, up_term = lax.psum((gate_part, up_part), "grp")
    hidden = (jax.nn.silu(gate_term) * up_term).astype(jnp.bfloat16)
    down_term = jnp.dot(hidden, w_down, preferred_element_type=jnp.float32)
    return (middle_part.astype(jnp.float32) + column_sum(down_term)).astype(jnp.bfloat16)


def solution(mesh):
    placed = (
        P(),
        P(),
        P(),
        P("grp", "rep", "tp", None),
        P("grp", "rep", "tp"),
        P("rep", "tp", None, "grp"),
        P("grp", ("tp", "rep")),
        P("grp", ("tp", "rep")),
        P(("tp", "rep"), "grp"),
        P(None, ("grp", "tp"), "rep", None),
        P(),
        P(),
    )
    return jax.shard_map(
        on_device,
        mesh=mesh,
        in_specs=placed,
        out_specs=P(None, ("grp", "tp", "rep")),
        check_vma=False,
    )
```

profile of v0, /device:TPU:1, one launch (start us, length us, event | category | flops | bytes accessed | tf_op | source)
XLA Modules:
  0.0 1152.9 jit_solution(4686427275193825868)
XLA Ops:
  6.6 1.2 multiply_reduce_fusion.2
  11.5 1.5 fusion.20
  13.1 1.2 fusion.26
  14.2 6.1 all-reduce.1
  20.4 69.1 %all-gather = bf16[32,160,8]{1,2,0:T(8,128)(2,1)S(1)} all-gather(bf16[1,160,8]{1,2,0:T(8,128)(2,1)S(1)} %maximum_bitcast_fusion), channel_id=1, replica_groups=mesh['grp'=2,'tp'=32,'rep'=2] {'tp'}, dimensions={0}, use_global_device_ids=true | all-gather | bytes 84480 | tf_op jit(solution)/shard_map/all_gather | solution.py:111
  91.1 5.4 fusion.59
  96.5 1.4 fusion.61
  98.8 1.3 fusion.16
  102.3 1.8 copy.52
  104.1 1.4 multiply_reduce_fusion
  105.7 1.4 fusion.24
  107.2 143.9 %all_gather.20 = bf16[64,8,32]{2,1,0:T(8,128)(2,1)S(1)} all-gather(bf16[1,8,32]{2,1,0:T(8,128)(2,1)S(1)} %convert_element_type.188), channel_id=1, replica_groups=mesh['grp'=2,'tp'=32,'rep'=2] {'grp','tp'}, dimensions={0}, use_global_device_ids=true | all-gather | bytes 33280 | tf_op jit(solution)/shard_map/all_gather | solution.py:13
  251.1 142.5 %all_gather.19 = bf16[64,8,32]{2,1,0:T(8,128)(2,1)S(1)} all-gather(bf16[1,8,32]{2,1,0:T(8,128)(2,1)S(1)} %convert_element_type.184), channel_id=1, replica_groups=mesh['grp'=2,'tp'=32,'rep'=2] {'grp','tp'}, dimensions={0}, use_global_device_ids=true | all-gather | bytes 33280 | tf_op jit(solution)/shard_map/all_gather | solution.py:13
  394.5 66.2 %while.19 = (s32[]{:T(128)}, f32[8,32]{1,0:T(8,128)S(1)}, f32[8,32]{1,0:T(8,128)S(1)}, f32[8,32,128]{2,1,0:T(8,128)S(1)}, bf16[64,8,32]{2,1,0:T(8,128)(2,1)S(1)}...) while((s32[]{:T(128)}, f32[8,32]{1,0:T(8,128)S(1)}, ...), condition=%wide.region_6.7_spmd, body=%wide.region_5.6_spmd.sunk | while | flops 133125 | bytes 337039 | solution.py:21
  394.5 1.0 fusion.68
  395.6 1.0 fusion.68
  396.6 1.0 fusion.68
  397.7 1.0 fusion.68
  398.7 1.0 fusion.68
  399.8 1.0 fusion.68
  400.9 1.0 fusion.68
  401.9 1.0 fusion.68
  403.0 1.0 fusion.68
  404.0 1.0 fusion.68
  405.1 1.0 fusion.68
  406.1 1.0 fusion.68
  407.2 1.0 fusion.68
  408.2 1.0 fusion.68
  417.7 1.0 fusion.68
  418.7 1.0 fusion.68
  419.8 1.0 fusion.68
  420.8 1.0 fusion.68
  421.9 1.0 fusion.68
  437.7 1.0 fusion.68
  438.7 1.0 fusion.68
  439.8 1.0 fusion.68
  440.8 1.0 fusion.68
  441.9 1.0 fusion.68
  457.6 1.0 fusion.68
  458.7 1.0 fusion.68
  459.7 1.0 fusion.68
  461.2 1.9 convolution_bitcast_fusion.1
  463.2 347.1 %reduce-scatter.7.cloned.1.call-done = f32[64,8]{1,0:T(8,128)} async-done(((f32[4096,8]{1,0:T(8,128)}), f32[64,8]{1,0:T(8,128)}) %reduce-scatter.7.cloned.1.call-update) | async-done | bytes 2064
  811.9 39.6 %all-gather.1 = bf16[128,64,8]{1,2,0:T(8,128)(2,1)S(1)} all-gather(bf16[1,64,8]{1,2,0:T(8,128)(2,1)S(1)} %bitcast.85), channel_id=1, replica_groups=mesh['grp'=2,'tp'=32,'rep'=2] {'grp','tp','rep'}, dimensions={0}, use_global_device_ids=true | all-gather | bytes 132096 | tf_op jit(solution)/shard_map/all_gather | solution.py:183
  852.3 2.2 fusion.54
  855.0 7.9 all-reduce
  862.9 2.3 convolution_bitcast_fusion
  865.3 279.7 %reduce-scatter.9.cloned.1.call-done = f32[64,8]{1,0:T(8,128)} async-done(((f32[4096,8]{1,0:T(8,128)}), f32[64,8]{1,0:T(8,128)}) %reduce-scatter.9.cloned.1.call-update) | async-done | bytes 2064
  (172 shorter events, 51.4 us)
Async XLA Ops:
  6.5 856.4 %copy-start = (bf16[224,4096]{1,0:T(8,128)(2,1)S(1)}, bf16[224,4096]{1,0:T(8,128)(2,1)}, u32[]{:S(2)}) copy-start(bf16[224,4096]{1,0:T(8,128)(2,1)} %param.22) | copy-start | bytes 5505028
  6.5 387.1 %all-gather.4.cloned.1.call-start = ((), (), s32[]{:S(2)}) async-start(), calls=%async_computation.2 | async-start | bytes 4259840 | tf_op jit(solution)/shard_map/all_gather | solution.py:13
  8.7 81.9 %copy-start.2 = (f32[8,8192]{1,0:T(8,128)}, f32[8,8192]{1,0:T(8,128)S(1)}, u32[]{:S(2)}) copy-start(f32[8,8192]{1,0:T(8,128)S(1)} %convert_element_type.177) | copy-start | bytes 786436
  98.0 0.8 copy-start.4
  100.2 710.1 %reduce-scatter.7.cloned.1.call-start = ((), (), s32[]{:S(2)}) async-start(), calls=%async_computation.3 | async-start | bytes 2129920
  105.5 355.7 %copy-start.3 = (bf16[1,1,128,4096]{3,2,1,0:T(8,128)(2,1)S(1)}, bf16[1,1,128,4096]{3,2,1,0:T(8,128)(2,1)}, u32[]{:S(2)}) copy-start(bf16[1,1,128,4096]{3,2,1,0:T(8,128)(2,1)} %param.19) | copy-start | bytes 3145732
  461.2 2.0 copy-start.5
  463.1 681.8 %reduce-scatter.9.cloned.1.call-start = ((), (), s32[]{:S(2)}) async-start(), calls=%async_computation.4 | async-start | bytes 2129920
  852.1 2.4 copy-start.1
Sparse Core Ops, SparseCore 0:
  100.3 79.5 all-gather.3
  463.3 346.9 reduce-scatter.6
  865.4 279.5 reduce-scatter.8
where the time goes:
time: 1160 us; the launch traced here: 1150 us
  waiting for transfers between devices  627 us (54%)
  blocking collectives  409 us (35%)
  other arithmetic  75.1 us (6%)
  local copies, waits for them, and re-layouts  13.8 us (1%)
  between operations  13.4 us (1%)
  matrix products  12.5 us (1%)
    unnamed x5, waiting for transfers between devices  627 us
    all_gather x2, blocking collectives, joined(): lax.all_gather(part.astype(kind), axis)  286 us
    all_gather x1, blocking collectives, on_device(): lax.all_gather(outgoing, 'tp', axis=1, tiled=True)  69.1 us
    add x63, other arithmetic, combine_parts(): left_num * left_scale[..., None] + right_num * right_scale[..., None]  63.1 us
    all_gather x1, blocking collectives, on_device(): lax.all_gather(middle_part, ('grp', 'tp', 'rep'), axis=1, tiled=True)  39.6 us
  transfers between devices with their start and end apart: 3, of which 2 were waited for; matrix products, arithmetic and copies ran while one was open for 1% of the time, Pallas kernels for 0%

commit v1 on v0

v1 whole, which is shorter than its diff:
```python
import functools
import math

import numpy as np
import jax
import jax.numpy as jnp
from jax import lax
from jax.sharding import PartitionSpec as P
import jax.experimental.pallas as pl
import jax.experimental.pallas.tpu as pltpu

MESH = pl.DeviceIdType.MESH
NT = (((1,), (1,)), ((), ()))
epsilon = 1e-05
base_freq = 500000.0
masked = -1e30
floor_peak = -1e20

REQ = 8
WIDTH = 8192
HALF = WIDTH // 2
TILES = HALF // 128
HD = 128
CTX_DEV = 512
HEADS = 32
N_TP = 32
PEERS = 64
UNITS = 224
FREQ = [
    float(f)
    for f in (base_freq ** (-(2.0 * np.arange(HD // 2, dtype=np.float64)) / HD)).astype(np.float32)
]


def swap_halves(tile, diagonal):
    turned = pltpu.roll(pltpu.roll(tile, 64, 1), 4, 0)
    return jnp.where(diagonal, tile, turned)


def layer(
    hidden_ref, attn_gain_ref, ffn_gain_ref, wq_ref, wkv_ref, wo_ref, wg_ref, wu_ref, wd_ref,
    kv_ref, len_ref, first_ref, out_ref,
    hid, gain_a, gain_f, wq, wkv, wo, wg, wu, wd, keys, values,
    send_a, recv_a, q_rot, stage_c, send_c, recv_c, send_d, recv_d, recv_e, send_f, recv_f,
    send_g, recv_g, x_ffn, load_sem, kv_sem, send_sem, recv_sem,
):
    g = lax.axis_index("grp")
    t = lax.axis_index("tp")
    r = lax.axis_index("rep")
    me_row = g * N_TP + t
    me_col = t * 2 + r

    def row_peer(k):
        p = (me_row + k) % PEERS
        return p, (p // N_TP, p % N_TP, r)

    def col_peer(k):
        p = (me_col + k) % PEERS
        return p, (g, p // 2, p % 2)

    own_half = pl.ds(pl.multiple_of(g * HALF, HALF), HALF)
    other_half = pl.ds(pl.multiple_of((1 - g) * HALF, HALF), HALF)
    loads = [
        (hidden_ref.at[:, own_half], hid.at[0]),
        (hidden_ref.at[:, other_half], hid.at[1]),
        (attn_gain_ref.at[:, own_half], gain_a),
        (wq_ref, wq),
        (wkv_ref, wkv),
        (ffn_gain_ref.at[:, own_half], gain_f),
        (wo_ref, wo),
        (wg_ref, wg),
        (wu_ref, wu),
        (wd_ref, wd),
    ]
    copies = [pltpu.make_async_copy(s, d, load_sem.at[i]) for i, (s, d) in enumerate(loads)]
    kv_copies = []
    for b in range(REQ):
        for i, dst in enumerate((keys, values)):
            kv_copies.append(
                pltpu.make_async_copy(
                    kv_ref.at[b, :, :, pl.ds(i * HD, HD)], dst.at[b], kv_sem.at[2 * b + i]
                )
            )
    for c in copies[:6] + kv_copies + copies[6:]:
        c.start()

    barrier = pltpu.get_barrier_semaphore()

    @pl.loop(1, PEERS)
    def _(k):
        _, dev = row_peer(k)
        pl.semaphore_signal(barrier, inc=1, device_id=dev, device_id_type=MESH)

    pl.semaphore_signal(barrier, inc=1, device_id=(g, t, 1 - r), device_id_type=MESH)

    for c in copies[:5]:
        c.wait()
    own = hid[0].astype(jnp.float32)
    other = hid[1].astype(jnp.float32)
    squares = jnp.sum(own * own, axis=1, keepdims=True) + jnp.sum(
        other * other, axis=1, keepdims=True
    )
    scale = lax.rsqrt(squares * (1.0 / WIDTH) + epsilon)
    normed = (own * scale * gain_a[...]).astype(jnp.bfloat16)
    query_part = jnp.dot(normed, wq[...], preferred_element_type=jnp.float32)
    keyval_part = lax.dot_general(normed, wkv[...], NT, preferred_element_type=jnp.float32)
    keyval_wide = jnp.concatenate(
        (keyval_part, jnp.zeros((REQ, HD - 32), jnp.float32)), axis=1
    )
    spot = t % 4
    placed = keyval_wide
    for s in range(1, 4):
        placed = jnp.where(spot == s, pltpu.roll(keyval_wide, 32 * s, 1), placed)
    message = jnp.concatenate((query_part, placed), axis=0).astype(jnp.bfloat16)
    send_a[...] = message
    recv_a[me_row] = message

    pl.semaphore_wait(barrier, PEERS)

    def send_all(peer, source, landing, stage):
        @pl.loop(1, PEERS)
        def _(k):
            p, dev = peer(k)
            pltpu.make_async_remote_copy(
                src_ref=source(p),
                dst_ref=landing,
                send_sem=send_sem.at[stage],
                recv_sem=recv_sem.at[stage],
                device_id=dev,
                device_id_type=MESH,
            ).start()

    def wait_all(buffer, sem):
        span = buffer.at[pl.ds(0, PEERS - 1)]
        pltpu.make_async_copy(span, span, sem).wait()

    send_all(row_peer, lambda p: send_a, recv_a.at[me_row], 0)

    lane8 = lax.broadcasted_iota(jnp.int32, (REQ, HD), 1)
    row8 = lax.broadcasted_iota(jnp.int32, (REQ, HD), 0)
    frequency = jnp.zeros((REQ, HD), jnp.float32)
    for i in range(HD // 2):
        frequency = jnp.where(lane8 // 2 == i, FREQ[i], frequency)
    position = jnp.zeros((REQ, HD), jnp.int32)
    for b in range(REQ):
        position = jnp.where(row8 == b, len_ref[b], position)
    angles = position.astype(jnp.float32) * frequency
    cos_part = jnp.cos(angles)
    sin_part = jnp.sin(angles)
    even = lane8 % 2 == 0
    sin_even = jnp.where(even, -sin_part, 0.0)
    sin_odd = jnp.where(even, 0.0, sin_part)

    def rotate(x):
        return (
            x * cos_part + pltpu.roll(x, HD - 1, 1) * sin_even + pltpu.roll(x, 1, 1) * sin_odd
        )

    rounded = lambda x: x.astype(jnp.bfloat16).astype(jnp.float32)
    lane_r = lax.broadcasted_iota(jnp.int32, (HEADS, 4 * CTX_DEV), 1)
    head_r = lax.broadcasted_iota(jnp.int32, (HEADS, 4 * CTX_DEV), 0)
    wrong_head = (lane_r % 4) != (head_r // 8)
    slot_lane = jnp.where(wrong_head, 4 * CTX_DEV, lane_r)
    lane_c = lax.broadcasted_iota(jnp.int32, (HEADS, HD), 1)
    diagonal = (lane8 < 64) == (row8 < 4)
    inv_scale = 1.0 / math.sqrt(HD)

    wait_all(recv_a, recv_sem.at[0])
    for head in range(HEADS):
        pair = recv_a[head].astype(jnp.float32) + recv_a[N_TP + head].astype(jnp.float32)
        q_rot[pl.ds(head * REQ, REQ), :] = rounded(rotate(rounded(pair[:REQ])))

    for b in range(REQ):
        kv_copies[2 * b].wait()
        kv_copies[2 * b + 1].wait()
        block = (me_row - first_ref[b]) & (PEERS - 1)
        live_rows = 4 * (len_ref[b] - block * CTX_DEV)
        q_b = q_rot[pl.ds(b, HEADS, stride=REQ), :].astype(jnp.bfloat16)
        k_b = keys[b].reshape(4 * CTX_DEV, HD)
        v_b = values[b].reshape(4 * CTX_DEV, HD)
        scores = lax.dot_general(q_b, k_b, NT, preferred_element_type=jnp.float32)
        scores = jnp.where(slot_lane < jnp.minimum(live_rows, 4 * CTX_DEV), scores * inv_scale, masked)
        peak = jnp.maximum(jnp.max(scores, axis=1, keepdims=True), floor_peak)
        peak_hi = rounded(peak)
        peak_lo = rounded(peak - peak_hi)
        weights = jnp.exp(scores - (peak_hi + peak_lo))
        total = jnp.sum(weights, axis=1, keepdims=True)
        total_hi = rounded(total)
        total_lo = rounded(total - total_hi)
        numerator = jnp.dot(weights.astype(jnp.bfloat16), v_b, preferred_element_type=jnp.float32)
        stats = jnp.where(
            lane_c < 64,
            jnp.where(lane_c < 32, peak_hi, peak_lo),
            jnp.where(lane_c < 96, total_hi, total_lo),
        )
        stage_c[pl.ds(b, HEADS, stride=16), :] = numerator
        stage_c[pl.ds(REQ + b, HEADS, stride=16), :] = stats
    for head in range(HEADS):
        send_c[head] = stage_c[pl.ds(head * 16, 16), :].astype(jnp.bfloat16)
    recv_c[me_row] = send_c[t]
    send_all(row_peer, lambda p: send_c.at[p % N_TP], recv_c.at[me_row], 1)

    kv_first = (t // 8) * 8
    new_key = jnp.zeros((REQ, HD), jnp.float32)
    new_value = jnp.zeros((REQ, HD), jnp.float32)
    for j in range(4):
        part = recv_a[kv_first + j].astype(jnp.float32) + recv_a[N_TP + kv_first + j].astype(
            jnp.float32
        )
        new_key = new_key + part[REQ:]
        part = recv_a[kv_first + 4 + j].astype(jnp.float32) + recv_a[
            N_TP + kv_first + 4 + j
        ].astype(jnp.float32)
        new_value = new_value + part[REQ:]
    key_rot = rounded(rotate(rounded(new_key)))
    new_value = rounded(new_value)
    my_query = q_rot[pl.ds(pl.multiple_of(t * REQ, REQ), REQ), :]
    own_score = jnp.sum(my_query * key_rot, axis=1, keepdims=True) * inv_scale
    pick_row = lax.broadcasted_iota(jnp.int32, (HD, 2 * HD), 0)
    pick_col = lax.broadcasted_iota(jnp.int32, (HD, 2 * HD), 1)
    pick = jnp.where(
        (pick_row % 32 == 0) & (pick_row // 64 == pick_col // HD), 1.0, 0.0
    ).astype(jnp.bfloat16)

    wait_all(recv_c, recv_sem.at[1])
    partial = recv_c[...]
    stats_all = partial.astype(jnp.float32)[:, REQ:, :].reshape(PEERS * REQ, HD).astype(jnp.bfloat16)
    spread = jnp.dot(stats_all, pick, preferred_element_type=jnp.float32)
    peaks = spread[:, :HD].reshape(PEERS, REQ, HD)
    totals = spread[:, HD:].reshape(PEERS, REQ, HD)
    top = jnp.maximum(jnp.max(peaks, axis=0), own_score)
    keep = jnp.exp(peaks - top[None])
    own_weight = jnp.exp(own_score - top)
    numer = jnp.sum(keep * partial.astype(jnp.float32)[:, :REQ, :], axis=0)
    denom = jnp.sum(keep * totals, axis=0) + own_weight
    attended = ((numer + rounded(own_weight) * new_value) / denom).astype(jnp.bfloat16)

    def scatter(send, recv, row, weight, stage):
        for i in range(TILES // 2):
            product = jnp.dot(
                row, weight[:, pl.ds(i * 256, 256)], preferred_element_type=jnp.float32
            )
            for j in range(2):
                tile = swap_halves(product[:, j * 128 : j * 128 + 128], diagonal)
                send[4 * i + 2 * j] = tile[:4]
                send[4 * i + 2 * j + 1] = tile[4:]
        recv[me_col] = send[me_col]
        send_all(col_peer, lambda p: send.at[p], recv.at[me_col], stage)

    copies[6].wait()
    scatter(send_d, recv_d, attended, wo, 2)
    my_column = pl.ds(pl.multiple_of(t * 128, 128), 128)
    my_hidden = swap_halves(hid[0, :, my_column].astype(jnp.float32), diagonal)
    my_hidden = jnp.where(r == 0, my_hidden[:4], my_hidden[4:])
    wait_all(recv_d, recv_sem.at[2])
    projected = jnp.sum(recv_d[...], axis=0)
    recv_e[me_col] = projected
    send_all(col_peer, lambda p: recv_e.at[me_col], recv_e.at[me_col], 3)
    my_middle = rounded(my_hidden + projected)
    for c in copies[5:6] + copies[7:]:
        c.wait()
    wait_all(recv_e, recv_sem.at[3])
    squares = jnp.zeros((REQ, HD), jnp.float32)
    for i in range(TILES):
        packed = jnp.concatenate((recv_e[2 * i], recv_e[2 * i + 1]), axis=0)
        col = pl.ds(i * 128, 128)
        middle = rounded(hid[0, :, col].astype(jnp.float32) + swap_halves(packed, diagonal))
        squares = squares + middle * middle
        x_ffn[:, col] = (middle * gain_f[:, col]).astype(jnp.bfloat16)

    x = x_ffn[...]
    gate_part = lax.dot_general(x, wg[...], NT, preferred_element_type=jnp.float32)
    up_part = lax.dot_general(x, wu[...], NT, preferred_element_type=jnp.float32)
    square_sum = jnp.broadcast_to(jnp.sum(squares, axis=1, keepdims=True), (REQ, 256 - UNITS))
    send_f[0] = jnp.concatenate((gate_part, square_sum), axis=1)
    send_f[1] = jnp.concatenate((up_part, square_sum), axis=1)
    swap = pltpu.make_async_remote_copy(
        src_ref=send_f,
        dst_ref=recv_f,
        send_sem=send_sem.at[4],
        recv_sem=recv_sem.at[4],
        device_id=(1 - g, t, r),
        device_id_type=MESH,
    )
    swap.start()
    swap.wait_recv()
    gate_sum = send_f[0] + recv_f[0]
    up_sum = send_f[1] + recv_f[1]
    scale = lax.rsqrt(gate_sum[:, UNITS : UNITS + 1] * (1.0 / WIDTH) + epsilon)
    gate = gate_sum[:, :UNITS] * scale
    up = up_sum[:, :UNITS] * scale
    active = (gate / (1.0 + jnp.exp(-gate)) * up).astype(jnp.bfloat16)

    scatter(send_g, recv_g, active, wd, 5)
    wait_all(recv_g, recv_sem.at[5])
    result = my_middle + jnp.sum(recv_g[...], axis=0)
    out_ref[...] = jnp.concatenate((result[:, :64], result[:, 64:]), axis=0).astype(out_ref.dtype)

    wait_all(recv_a, send_sem.at[0])
    wait_all(recv_c, send_sem.at[1])
    wait_all(recv_d, send_sem.at[2])
    wait_all(recv_e, send_sem.at[3])
    swap.wait_send()
    wait_all(recv_g, send_sem.at[5])


def on_device(
    hidden_states, attn_gain, ffn_gain, w_query, w_keyval, w_out, w_gate, w_up, w_down,
    kv_cache, lengths, first_shard,
):
    anywhere = pl.BlockSpec(memory_space=pl.ANY)
    scalars = pl.BlockSpec(memory_space=pltpu.SMEM)
    f32, bf16 = jnp.float32, jnp.bfloat16
    return pl.pallas_call(
        layer,
        out_shape=jax.ShapeDtypeStruct((REQ, 64), bf16),
        in_specs=[anywhere] * 10 + [scalars] * 2,
        out_specs=pl.BlockSpec(memory_space=pltpu.VMEM),
        scratch_shapes=[
            pltpu.VMEM((2, REQ, HALF), bf16),
            pltpu.VMEM((1, HALF), f32),
            pltpu.VMEM((1, HALF), f32),
            pltpu.VMEM((HALF, HD), bf16),
            pltpu.VMEM((32, HALF), bf16),
            pltpu.VMEM((HD, HALF), bf16),
            pltpu.VMEM((UNITS, HALF), bf16),
            pltpu.VMEM((UNITS, HALF), bf16),
            pltpu.VMEM((UNITS, HALF), bf16),
            pltpu.VMEM((REQ, CTX_DEV, 4, HD), bf16),
            pltpu.VMEM((REQ, CTX_DEV, 4, HD), bf16),
            pltpu.VMEM((16, HD), bf16),
            pltpu.VMEM((PEERS, 16, HD), bf16),
            pltpu.VMEM((HEADS * REQ, HD), f32),
            pltpu.VMEM((HEADS * 16, HD), f32),
            pltpu.VMEM((HEADS, 16, HD), bf16),
            pltpu.VMEM((PEERS, 16, HD), bf16),
            pltpu.VMEM((PEERS, 4, HD), f32),
            pltpu.VMEM((PEERS, 4, HD), f32),
            pltpu.VMEM((PEERS, 4, HD), f32),
            pltpu.VMEM((2, REQ, 256), f32),
            pltpu.VMEM((2, REQ, 256), f32),
            pltpu.VMEM((PEERS, 4, HD), f32),
            pltpu.VMEM((PEERS, 4, HD), f32),
            pltpu.VMEM((REQ, HALF), bf16),
            pltpu.SemaphoreType.DMA((10,)),
            pltpu.SemaphoreType.DMA((2 * REQ,)),
            pltpu.SemaphoreType.DMA((6,)),
            pltpu.SemaphoreType.DMA((6,)),
        ],
        compiler_params=pltpu.CompilerParams(
            collective_id=0, has_side_effects=True, vmem_limit_bytes=48 << 20
        ),
    )(
        hidden_states,
        attn_gain.reshape(1, WIDTH),
        ffn_gain.reshape(1, WIDTH),
        w_query.reshape(HALF, HD),
        w_keyval.reshape(HALF, 32).T,
        w_out.reshape(HD, HALF),
        w_gate.T,
        w_up.T,
        w_down,
        kv_cache,
        lengths,
        first_shard,
    )


def solution(mesh):
    placed = (
        P(),
        P(),
        P(),
        P("grp", "rep", "tp", None),
        P("grp", "rep", "tp"),
        P("rep", "tp", None, "grp"),
        P("grp", ("tp", "rep")),
        P("grp", ("tp", "rep")),
        P(("tp", "rep"), "grp"),
        P(None, ("grp", "tp"), "rep", None),
        P(),
        P(),
    )
    return jax.shard_map(
        on_device,
        mesh=mesh,
        in_specs=placed,
        out_specs=P(None, ("grp", "tp", "rep")),
        check_vma=False,
    )
```

time: 1160 us -> 63.6 us (0.05)
  waiting for transfers between devices: 627 us -> 0 us
  blocking collectives: 409 us -> 0 us
  other arithmetic: 75.1 us -> 0 us
  Pallas kernels: 0 us -> 53.9 us
  between operations: 13.4 us -> 0.02 us
  matrix products: 12.5 us -> 0 us
    unnamed x5 -> x0, waiting for transfers between devices: 627 us -> none
    all_gather x4 -> x0, blocking collectives: 395 us -> none  [the longest x2 286 us: joined(): lax.all_gather(part.astype(kind), axis)]
    add x126 -> x0, other arithmetic: 64.3 us -> none  [the longest x63 63.1 us: combine_parts(): left_num * left_scale[..., None] + right_num * right_scale[..., None]]
    pallas_call x0 -> x1, Pallas kernels: none -> 53.9 us  [on_device(): pl.pallas_call(layer, out_shape=jax.ShapeDtypeStruct((REQ, 64), bf16), in...]
    psum x2 -> x0, blocking collectives: 14 us -> none  [the longest x1 7.89 us: on_device(): gate_term, up_term = lax.psum((gate_part, up_part), 'grp')]
  transfers between devices with their start and end apart: 3 -> 0, of which waited for: 2 -> 0; matrix products, arithmetic and copies ran while one was open for 1% -> 0% of each run, Pallas kernels for 0% -> 0%
where the time goes in v1:
time: 63.6 us; the launch traced here: 63.1 us
  Pallas kernels  53.9 us (85%)
  local copies, waits for them, and re-layouts  9.21 us (14%)
    pallas_call x1, Pallas kernels, on_device(): pl.pallas_call(layer, out_shape=jax.ShapeDtypeStruct((REQ, 64), bf16), in...  53.9 us
    unnamed x19, local copies, waits for them, and re-layouts  9.21 us

profile of v1, /device:TPU:1, one launch (start us, length us, event | category | flops | bytes accessed | tf_op | source)
XLA Modules:
  0.0 63.1 jit_solution(6113726696945954829)
XLA Ops:
  0.0 0.0 copy-start
  0.0 1.5 %copy-done = bf16[4096,224]{0,1:T(8,128)(2,1)S(1)} copy-done((bf16[4096,224]{0,1:T(8,128)(2,1)S(1)}, bf16[4096,224]{0,1:T(8,128)(2,1)}, u32[]{:S(2)}) %copy-start) | copy-done | bytes 1835032
  1.5 0.0 copy-start.1
  1.5 1.2 %copy-done.1 = bf16[4096,1,1,128]{3,0,2,1:T(8,128)(2,1)S(1)} copy-done((bf16[4096,1,1,128]{3,0,2,1:T(8,128)(2,1)S(1)}, bf16[4096,1,1,128]{3,0,2,1:T(8,128)(2,1)}, u32[]{:S(2)}) %copy-start.1) | copy-done | bytes 1048600
  2.7 0.0 copy-start.2
  2.7 1.2 %copy-done.2 = bf16[1,1,128,4096]{3,2,1,0:T(8,128)(2,1)S(1)} copy-done((bf16[1,1,128,4096]{3,2,1,0:T(8,128)(2,1)S(1)}, bf16[1,1,128,4096]{3,2,1,0:T(8,128)(2,1)}, u32[]{:S(2)}) %copy-start.2) | copy-done | bytes 1048600
  4.0 0.0 copy-start.3
  4.0 0.9 %copy-done.3 = bf16[4096,1,32]{0,2,1:T(8,128)(2,1)S(1)} copy-done((bf16[4096,1,32]{0,2,1:T(8,128)(2,1)S(1)}, bf16[4096,1,32]{0,2,1:T(8,128)(2,1)}, u32[]{:S(2)}) %copy-start.3) | copy-done | bytes 262168
  4.9 0.0 copy-start.4
  4.9 0.9 %copy-done.4 = bf16[8,8192]{1,0:T(8,128)(2,1)S(1)} copy-done((bf16[8,8192]{1,0:T(8,128)(2,1)S(1)}, bf16[8,8192]{1,0:T(8,128)(2,1)}, u32[]{:S(2)}) %copy-start.4) | copy-done | bytes 131096
  5.8 0.0 copy-start.5
  5.8 0.8 %copy-done.5 = f32[8192]{0:T(1024)S(1)} copy-done((f32[8192]{0:T(1024)S(1)}, f32[8192]{0:T(1024)}, u32[]{:S(2)}) %copy-start.5) | copy-done | bytes 32792
  6.6 0.0 copy-start.6
  6.6 0.8 %copy-done.6 = f32[8192]{0:T(1024)S(1)} copy-done((f32[8192]{0:T(1024)S(1)}, f32[8192]{0:T(1024)}, u32[]{:S(2)}) %copy-start.6) | copy-done | bytes 32792
  7.3 0.0 copy-start.7
  7.3 0.7 %copy-done.7 = s32[8]{0:T(128)S(1)} copy-done((s32[8]{0:T(128)S(1)}, s32[8]{0:T(128)}, u32[]{:S(2)}) %copy-start.7) | copy-done | bytes 56
  8.0 0.0 copy-start.8
  8.0 0.7 %copy-done.8 = s32[8]{0:T(128)S(1)} copy-done((s32[8]{0:T(128)S(1)}, s32[8]{0:T(128)}, u32[]{:S(2)}) %copy-start.8) | copy-done | bytes 56
  8.6 53.9 %shard_map.118 = bf16[8,64]{1,0:T(8,128)(2,1)S(1)} custom-call(bf16[8,8192]{1,0:T(8,128)(2,1)S(1)} %copy-done.4, f32[1,8192]{1,0:T(1,128)S(1)} %bitcast.13, f32[1,8192]{1,0:T(1,128)S(1)} %bitcast.14, bf16[4096,128]{1,0:T(8,128)(2,1)S(1)} %bitcast.10, bf16[32,4096]{1,0:T(8,128)(2,1)S(1)} %bitcast.12, bf16[128,4096]{1,0:T(8,128)(2,1)S(1)} %bitcast.11, ...), custom_call_target="tpu_custom_call" | custom-call | tf_op jit(solution)/shard_map/pallas_call | solution.py:314
  62.6 0.6 copy.14
Async XLA Ops:
  0.0 1.5 %copy-start = (bf16[4096,224]{0,1:T(8,128)(2,1)S(1)}, bf16[4096,224]{0,1:T(8,128)(2,1)}, u32[]{:S(2)}) copy-start(bf16[4096,224]{0,1:T(8,128)(2,1)} %param.18) | copy-start | bytes 5505028
  1.5 1.2 %copy-start.1 = (bf16[4096,1,1,128]{3,0,2,1:T(8,128)(2,1)S(1)}, bf16[4096,1,1,128]{3,0,2,1:T(8,128)(2,1)}, u32[]{:S(2)}) copy-start(bf16[4096,1,1,128]{3,0,2,1:T(8,128)(2,1)} %param.15) | copy-start | bytes 3145732
  2.7 1.2 %copy-start.2 = (bf16[1,1,128,4096]{3,2,1,0:T(8,128)(2,1)S(1)}, bf16[1,1,128,4096]{3,2,1,0:T(8,128)(2,1)}, u32[]{:S(2)}) copy-start(bf16[1,1,128,4096]{3,2,1,0:T(8,128)(2,1)} %param.17) | copy-start | bytes 3145732
  4.0 0.9 %copy-start.3 = (bf16[4096,1,32]{0,2,1:T(8,128)(2,1)S(1)}, bf16[4096,1,32]{0,2,1:T(8,128)(2,1)}, u32[]{:S(2)}) copy-start(bf16[4096,1,32]{0,2,1:T(8,128)(2,1)} %param.16) | copy-start | bytes 786436
  4.9 0.9 %copy-start.4 = (bf16[8,8192]{1,0:T(8,128)(2,1)S(1)}, bf16[8,8192]{1,0:T(8,128)(2,1)}, u32[]{:S(2)}) copy-start(bf16[8,8192]{1,0:T(8,128)(2,1)} %hidden_ref.1) | copy-start | bytes 393220
  5.8 0.8 %copy-start.5 = (f32[8192]{0:T(1024)S(1)}, f32[8192]{0:T(1024)}, u32[]{:S(2)}) copy-start(f32[8192]{0:T(1024)} %param.13) | copy-start | bytes 98308
  6.6 0.8 %copy-start.6 = (f32[8192]{0:T(1024)S(1)}, f32[8192]{0:T(1024)}, u32[]{:S(2)}) copy-start(f32[8192]{0:T(1024)} %param.14) | copy-start | bytes 98308
  7.3 0.7 %copy-start.7 = (s32[8]{0:T(128)S(1)}, s32[8]{0:T(128)}, u32[]{:S(2)}) copy-start(s32[8]{0:T(128)} %len_ref.1) | copy-start | bytes 100
  8.0 0.7 %copy-start.8 = (s32[8]{0:T(128)S(1)}, s32[8]{0:T(128)}, u32[]{:S(2)}) copy-start(s32[8]{0:T(128)} %first_ref.1) | copy-start | bytes 100

commit v2 on v1

--- a/solution.py
+++ b/solution.py
@@ -39,8 +39,8 @@
 
 def layer(
     hidden_ref, attn_gain_ref, ffn_gain_ref, wq_ref, wkv_ref, wo_ref, wg_ref, wu_ref, wd_ref,
-    kv_ref, len_ref, first_ref, out_ref,
-    hid, gain_a, gain_f, wq, wkv, wo, wg, wu, wd, keys, values,
+    kv_ref, lengths_ref, first_shard_ref, out_ref,
+    len_ref, first_ref, hid, gain_a, gain_f, wq, wkv, wo, wg, wu, wd, w_in, keys, keys_t, values,
     send_a, recv_a, q_rot, stage_c, send_c, recv_c, send_d, recv_d, recv_e, send_f, recv_f,
     send_g, recv_g, x_ffn, load_sem, kv_sem, send_sem, recv_sem,
 ):
@@ -50,13 +50,27 @@
     me_row = g * N_TP + t
     me_col = t * 2 + r
 
+    y, x, z = me_row // 16, (t // 4) % 4, t % 4
+
+    def far_first(i):
+        return 2 + i - (i // 2) * (2 * i - 1)
+
     def row_peer(k):
-        p = (me_row + k) % PEERS
-        return p, (p // N_TP, p % N_TP, r)
+        there = (me_row + 1 + k) % PEERS
+        return there, (there // N_TP, there % N_TP, r)
 
     def col_peer(k):
-        p = (me_col + k) % PEERS
-        return p, (g, p // 2, p % 2)
+        there = (me_col + 1 + k) % PEERS
+        return there, (g, there // 2, there % 2)
+
+    barrier = pltpu.get_barrier_semaphore()
+
+    @pl.loop(0, PEERS - 1)
+    def _(k):
+        _, dev = row_peer(k)
+        pl.semaphore_signal(barrier, inc=1, device_id=dev, device_id_type=MESH)
+
+    pl.semaphore_signal(barrier, inc=1, device_id=(g, t, 1 - r), device_id_type=MESH)
 
     own_half = pl.ds(pl.multiple_of(g * HALF, HALF), HALF)
     other_half = pl.ds(pl.multiple_of((1 - g) * HALF, HALF), HALF)
@@ -71,30 +85,26 @@
         (wg_ref, wg),
         (wu_ref, wu),
         (wd_ref, wd),
+        (lengths_ref, len_ref),
+        (first_shard_ref, first_ref),
     ]
     copies = [pltpu.make_async_copy(s, d, load_sem.at[i]) for i, (s, d) in enumerate(loads)]
+    kv_rows = kv_ref.reshape(REQ, 4 * CTX_DEV, 2 * HD)
     kv_copies = []
     for b in range(REQ):
         for i, dst in enumerate((keys, values)):
             kv_copies.append(
                 pltpu.make_async_copy(
-                    kv_ref.at[b, :, :, pl.ds(i * HD, HD)], dst.at[b], kv_sem.at[2 * b + i]
+                    kv_rows.at[b, :, pl.ds(i * HD, HD)], dst.at[b], kv_sem.at[2 * b + i]
                 )
             )
-    for c in copies[:6] + kv_copies + copies[6:]:
+    for c in copies[:5] + copies[10:]:
         c.start()
-
-    barrier = pltpu.get_barrier_semaphore()
-
-    @pl.loop(1, PEERS)
-    def _(k):
-        _, dev = row_peer(k)
-        pl.semaphore_signal(barrier, inc=1, device_id=dev, device_id_type=MESH)
-
-    pl.semaphore_signal(barrier, inc=1, device_id=(g, t, 1 - r), device_id_type=MESH)
 
     for c in copies[:5]:
         c.wait()
+    for c in kv_copies[::2] + kv_copies[1::2] + copies[5:10]:
+        c.start()
     own = hid[0].astype(jnp.float32)
     other = hid[1].astype(jnp.float32)
     squares = jnp.sum(own * own, axis=1, keepdims=True) + jnp.sum(
@@ -118,7 +128,7 @@
     pl.semaphore_wait(barrier, PEERS)
 
     def send_all(peer, source, landing, stage):
-        @pl.loop(1, PEERS)
+        @pl.loop(0, PEERS - 1)
         def _(k):
             p, dev = peer(k)
             pltpu.make_async_remote_copy(
@@ -142,6 +152,8 @@
     for i in range(HD // 2):
         frequency = jnp.where(lane8 // 2 == i, FREQ[i], frequency)
     position = jnp.zeros((REQ, HD), jnp.int32)
+    for c in copies[10:]:
+        c.wait()
     for b in range(REQ):
         position = jnp.where(row8 == b, len_ref[b], position)
     angles = position.astype(jnp.float32) * frequency
@@ -157,49 +169,84 @@
         )
 
     rounded = lambda x: x.astype(jnp.bfloat16).astype(jnp.float32)
-    lane_r = lax.broadcasted_iota(jnp.int32, (HEADS, 4 * CTX_DEV), 1)
-    head_r = lax.broadcasted_iota(jnp.int32, (HEADS, 4 * CTX_DEV), 0)
-    wrong_head = (lane_r % 4) != (head_r // 8)
-    slot_lane = jnp.where(wrong_head, 4 * CTX_DEV, lane_r)
-    lane_c = lax.broadcasted_iota(jnp.int32, (HEADS, HD), 1)
+    lane_row = lax.broadcasted_iota(jnp.int32, (REQ, 4 * CTX_DEV), 1)
+    of_kv_head = [lane_row % 4 == i for i in range(4)]
+    quarter = lane8 // 32
     diagonal = (lane8 < 64) == (row8 < 4)
     inv_scale = 1.0 / math.sqrt(HD)
+
+    for b in range(REQ):
+        kv_copies[2 * b].wait()
+        keys_t[b] = keys[b].T
 
     wait_all(recv_a, recv_sem.at[0])
     for head in range(HEADS):
         pair = recv_a[head].astype(jnp.float32) + recv_a[N_TP + head].astype(jnp.float32)
         q_rot[pl.ds(head * REQ, REQ), :] = rounded(rotate(rounded(pair[:REQ])))
 
-    for b in range(REQ):
-        kv_copies[2 * b].wait()
-        kv_copies[2 * b + 1].wait()
+    def spread(row, op):
+        for shift in (4, 8, 16, 32, 64):
+            row = op(row, pltpu.roll(row, shift, 1))
+        return row
+
+    scores = []
+    for b in range(REQ):
+        q_b = q_rot[pl.ds(b, HEADS, stride=REQ), :].astype(jnp.bfloat16)
+        scores.append(jnp.dot(q_b, keys_t[b], preferred_element_type=jnp.float32))
+    weights = []
+    for b in range(REQ):
         block = (me_row - first_ref[b]) & (PEERS - 1)
         live_rows = 4 * (len_ref[b] - block * CTX_DEV)
-        q_b = q_rot[pl.ds(b, HEADS, stride=REQ), :].astype(jnp.bfloat16)
-        k_b = keys[b].reshape(4 * CTX_DEV, HD)
-        v_b = values[b].reshape(4 * CTX_DEV, HD)
-        scores = lax.dot_general(q_b, k_b, NT, preferred_element_type=jnp.float32)
-        scores = jnp.where(slot_lane < jnp.minimum(live_rows, 4 * CTX_DEV), scores * inv_scale, masked)
-        peak = jnp.maximum(jnp.max(scores, axis=1, keepdims=True), floor_peak)
+        grid = [scores[b][8 * i : 8 * i + 8] for i in range(4)]
+        score = jnp.where(
+            of_kv_head[0],
+            grid[0],
+            jnp.where(of_kv_head[1], grid[1], jnp.where(of_kv_head[2], grid[2], grid[3])),
+        )
+        score = jnp.where(lane_row < live_rows, score * inv_scale, masked)
+        peak = functools.reduce(
+            jnp.maximum, [score[:, HD * i : HD * i + HD] for i in range(4 * CTX_DEV // HD)]
+        )
+        peak = jnp.maximum(spread(peak, jnp.maximum), floor_peak)
         peak_hi = rounded(peak)
         peak_lo = rounded(peak - peak_hi)
-        weights = jnp.exp(scores - (peak_hi + peak_lo))
-        total = jnp.sum(weights, axis=1, keepdims=True)
+        base = peak_hi + peak_lo
+        weight = jnp.exp(score - jnp.concatenate([base] * (4 * CTX_DEV // HD), axis=1))
+        total = functools.reduce(
+            jnp.add, [weight[:, HD * i : HD * i + HD] for i in range(4 * CTX_DEV // HD)]
+        )
+        total = spread(total, jnp.add)
         total_hi = rounded(total)
         total_lo = rounded(total - total_hi)
-        numerator = jnp.dot(weights.astype(jnp.bfloat16), v_b, preferred_element_type=jnp.float32)
         stats = jnp.where(
-            lane_c < 64,
-            jnp.where(lane_c < 32, peak_hi, peak_lo),
-            jnp.where(lane_c < 96, total_hi, total_lo),
-        )
-        stage_c[pl.ds(b, HEADS, stride=16), :] = numerator
-        stage_c[pl.ds(REQ + b, HEADS, stride=16), :] = stats
+            quarter < 2,
+            jnp.where(quarter == 0, peak_hi, peak_lo),
+            jnp.where(quarter == 2, total_hi, total_lo),
+        )
+        for i in range(4):
+            stage_c[pl.ds(REQ + b + 16 * 8 * i, 8, stride=16), :] = stats
+        weights.append(
+            jnp.concatenate(
+                [jnp.where(of_kv_head[i], weight, 0.0) for i in range(4)], axis=0
+            ).astype(jnp.bfloat16)
+        )
+    for b in range(REQ):
+        kv_copies[2 * b + 1].wait()
+    for b in range(REQ):
+        stage_c[pl.ds(b, HEADS, stride=16), :] = jnp.dot(
+            weights[b], values[b], preferred_element_type=jnp.float32
+        )
     for head in range(HEADS):
         send_c[head] = stage_c[pl.ds(head * 16, 16), :].astype(jnp.bfloat16)
     recv_c[me_row] = send_c[t]
     send_all(row_peer, lambda p: send_c.at[p % N_TP], recv_c.at[me_row], 1)
 
+    for c in copies[7:9]:
+        c.wait()
+    for first in (UNITS, 256 + UNITS):
+        w_in[:, first : first + 256 - UNITS] = jnp.zeros((HALF, 256 - UNITS), jnp.bfloat16)
+    w_in[:, :UNITS] = wg[...].T
+    w_in[:, 256 : 256 + UNITS] = wu[...].T
     kv_first = (t // 8) * 8
     new_key = jnp.zeros((REQ, HD), jnp.float32)
     new_value = jnp.zeros((REQ, HD), jnp.float32)
@@ -219,7 +266,7 @@
     pick_row = lax.broadcasted_iota(jnp.int32, (HD, 2 * HD), 0)
     pick_col = lax.broadcasted_iota(jnp.int32, (HD, 2 * HD), 1)
     pick = jnp.where(
-        (pick_row % 32 == 0) & (pick_row // 64 == pick_col // HD), 1.0, 0.0
+        (pick_row % 32 == t // 8) & (pick_row // 64 == pick_col // HD), 1.0, 0.0
     ).astype(jnp.bfloat16)
 
     wait_all(recv_c, recv_sem.at[1])
@@ -257,7 +304,7 @@
     recv_e[me_col] = projected
     send_all(col_peer, lambda p: recv_e.at[me_col], recv_e.at[me_col], 3)
     my_middle = rounded(my_hidden + projected)
-    for c in copies[5:6] + copies[7:]:
+    for c in copies[5:6] + copies[9:10]:
         c.wait()
     wait_all(recv_e, recv_sem.at[3])
     squares = jnp.zeros((REQ, HD), jnp.float32)
@@ -268,9 +315,9 @@
         squares = squares + middle * middle
         x_ffn[:, col] = (middle * gain_f[:, col]).astype(jnp.bfloat16)
 
-    x = x_ffn[...]
-    gate_part = lax.dot_general(x, wg[...], NT, preferred_element_type=jnp.float32)
-    up_part = lax.dot_general(x, wu[...], NT, preferred_element_type=jnp.float32)
+    product = jnp.dot(x_ffn[...], w_in[...], preferred_element_type=jnp.float32)
+    gate_part = product[:, :UNITS]
+    up_part = product[:, 256 : 256 + UNITS]
     square_sum = jnp.broadcast_to(jnp.sum(squares, axis=1, keepdims=True), (REQ, 256 - UNITS))
     send_f[0] = jnp.concatenate((gate_part, square_sum), axis=1)
     send_f[1] = jnp.concatenate((up_part, square_sum), axis=1)
@@ -308,15 +355,16 @@
     hidden_states, attn_gain, ffn_gain, w_query, w_keyval, w_out, w_gate, w_up, w_down,
     kv_cache, lengths, first_shard,
 ):
-    anywhere = pl.BlockSpec(memory_space=pl.ANY)
-    scalars = pl.BlockSpec(memory_space=pltpu.SMEM)
+    outside = pl.BlockSpec(memory_space=pltpu.HBM)
     f32, bf16 = jnp.float32, jnp.bfloat16
     return pl.pallas_call(
         layer,
         out_shape=jax.ShapeDtypeStruct((REQ, 64), bf16),
-        in_specs=[anywhere] * 10 + [scalars] * 2,
+        in_specs=[outside] * 12,
         out_specs=pl.BlockSpec(memory_space=pltpu.VMEM),
         scratch_shapes=[
+            pltpu.SMEM((REQ,), jnp.int32),
+            pltpu.SMEM((REQ,), jnp.int32),
             pltpu.VMEM((2, REQ, HALF), bf16),
             pltpu.VMEM((1, HALF), f32),
             pltpu.VMEM((1, HALF), f32),
@@ -326,8 +374,10 @@
             pltpu.VMEM((UNITS, HALF), bf16),
             pltpu.VMEM((UNITS, HALF), bf16),
             pltpu.VMEM((UNITS, HALF), bf16),
-            pltpu.VMEM((REQ, CTX_DEV, 4, HD), bf16),
-            pltpu.VMEM((REQ, CTX_DEV, 4, HD), bf16),
+            pltpu.VMEM((HALF, 512), bf16),
+            pltpu.VMEM((REQ, 4 * CTX_DEV, HD), bf16),
+            pltpu.VMEM((REQ, HD, 4 * CTX_DEV), bf16),
+            pltpu.VMEM((REQ, 4 * CTX_DEV, HD), bf16),
             pltpu.VMEM((16, HD), bf16),
             pltpu.VMEM((PEERS, 16, HD), bf16),
             pltpu.VMEM((HEADS * REQ, HD), f32),
@@ -342,13 +392,13 @@
             pltpu.VMEM((PEERS, 4, HD), f32),
             pltpu.VMEM((PEERS, 4, HD), f32),
             pltpu.VMEM((REQ, HALF), bf16),
-            pltpu.SemaphoreType.DMA((10,)),
+            pltpu.SemaphoreType.DMA((12,)),
             pltpu.SemaphoreType.DMA((2 * REQ,)),
             pltpu.SemaphoreType.DMA((6,)),
             pltpu.SemaphoreType.DMA((6,)),
         ],
         compiler_params=pltpu.CompilerParams(
-            collective_id=0, has_side_effects=True, vmem_limit_bytes=48 << 20
+            collective_id=0, has_side_effects=True, vmem_limit_bytes=60 << 20
         ),
     )(
         hidden_states,

time: 63.6 us -> 51.7 us (0.81)
  local copies, waits for them, and re-layouts: 9.21 us -> 1.26 us
  Pallas kernels: 53.9 us -> 50.3 us
    unnamed x19 -> x1, local copies, waits for them, and re-layouts: 9.21 us -> 1.26 us
    pallas_call x1, Pallas kernels: 53.9 us -> 50.3 us  [on_device(): pl.pallas_call(layer, out_shape=jax.ShapeDtypeStruct((REQ, 64), bf16), in...]
where the time goes in v2:
time: 51.7 us; the launch traced here: 51.6 us
  Pallas kernels  50.3 us (97%)
  local copies, waits for them, and re-layouts  1.26 us (2%)
    pallas_call x1, Pallas kernels, on_device(): pl.pallas_call(layer, out_shape=jax.ShapeDtypeStruct((REQ, 64), bf16), in...  50.3 us
    unnamed x1, local copies, waits for them, and re-layouts  1.26 us

profile of v2, /device:TPU:1, one launch (start us, length us, event | category | flops | bytes accessed | tf_op | source)
XLA Modules:
  0.0 51.6 jit_solution(15245552909109033255)
XLA Ops:
  0.0 50.3 %shard_map.118 = bf16[8,64]{1,0:T(8,128)(2,1)} custom-call(bf16[8,8192]{1,0:T(8,128)(2,1)} %hidden_ref.1, f32[1,8192]{1,0:T(1,128)} %bitcast.14, f32[1,8192]{1,0:T(1,128)} %bitcast.15, bf16[4096,128]{1,0:T(8,128)(2,1)} %bitcast.11, bf16[32,4096]{1,0:T(8,128)(2,1)} %bitcast.13, bf16[128,4096]{1,0:T(8,128)(2,1)} %bitcast.12, bf16[224,4096]{1,0:T(8,128)(2,1)} %bitcast.9, ...), custom_call_target="tpu_custom_call" | custom-call | tf_op jit(solution)/shard_map/pallas_call | solution.py:360
  50.3 1.3 %copy.14 = bf16[8,64]{1,0:T(8,128)(2,1)} copy(bf16[8,64]{1,0:T(8,128)(2,1)} %shard_map.118) | data formatting | bytes 2048

commit v3 on v2

--- a/solution.py
+++ b/solution.py
@@ -25,6 +25,7 @@
 HEADS = 32
 N_TP = 32
 PEERS = 64
+KV_PEERS = 16
 UNITS = 224
 FREQ = [
     float(f)
@@ -41,7 +42,7 @@
     hidden_ref, attn_gain_ref, ffn_gain_ref, wq_ref, wkv_ref, wo_ref, wg_ref, wu_ref, wd_ref,
     kv_ref, lengths_ref, first_shard_ref, out_ref,
     len_ref, first_ref, hid, gain_a, gain_f, wq, wkv, wo, wg, wu, wd, w_in, keys, keys_t, values,
-    send_a, recv_a, q_rot, stage_c, send_c, recv_c, send_d, recv_d, recv_e, send_f, recv_f,
+    send_a, recv_a, recv_kv, q_rot, stage_c, send_c, recv_c, send_d, recv_d, recv_e, send_f, recv_f,
     send_g, recv_g, x_ffn, load_sem, kv_sem, send_sem, recv_sem,
 ):
     g = lax.axis_index("grp")
@@ -59,13 +60,19 @@
         there = (me_row + 1 + k) % PEERS
         return there, (there // N_TP, there % N_TP, r)
 
+    me_kv = g * 8 + t % 8
+
+    def kv_peer(k):
+        there = (me_kv + 1 + k) % KV_PEERS
+        return there, (there // 8, (t // 8) * 8 + there % 8, r)
+
     def col_peer(k):
         there = (me_col + 1 + k) % PEERS
         return there, (g, there // 2, there % 2)
 
     barrier = pltpu.get_barrier_semaphore()
 
-    @pl.loop(0, PEERS - 1)
+    @pl.loop(0, PEERS - 1, unroll=True)
     def _(k):
         _, dev = row_peer(k)
         pl.semaphore_signal(barrier, inc=1, device_id=dev, device_id_type=MESH)
@@ -121,14 +128,15 @@
     placed = keyval_wide
     for s in range(1, 4):
         placed = jnp.where(spot == s, pltpu.roll(keyval_wide, 32 * s, 1), placed)
-    message = jnp.concatenate((query_part, placed), axis=0).astype(jnp.bfloat16)
-    send_a[...] = message
-    recv_a[me_row] = message
+    send_a[0] = query_part.astype(jnp.bfloat16)
+    recv_a[me_row] = send_a[0]
+    send_a[1] = placed.astype(jnp.bfloat16)
+    recv_kv[me_kv] = send_a[1]
 
     pl.semaphore_wait(barrier, PEERS)
 
-    def send_all(peer, source, landing, stage):
-        @pl.loop(0, PEERS - 1)
+    def send_all(peer, source, landing, stage, peers=PEERS):
+        @pl.loop(0, peers - 1)
         def _(k):
             p, dev = peer(k)
             pltpu.make_async_remote_copy(
@@ -140,11 +148,12 @@
                 device_id_type=MESH,
             ).start()
 
-    def wait_all(buffer, sem):
-        span = buffer.at[pl.ds(0, PEERS - 1)]
+    def wait_all(buffer, sem, peers=PEERS):
+        span = buffer.at[pl.ds(0, peers - 1)]
         pltpu.make_async_copy(span, span, sem).wait()
 
-    send_all(row_peer, lambda p: send_a, recv_a.at[me_row], 0)
+    send_all(row_peer, lambda p: send_a.at[0], recv_a.at[me_row], 0)
+    send_all(kv_peer, lambda p: send_a.at[1], recv_kv.at[me_kv], 6, KV_PEERS)
 
     lane8 = lax.broadcasted_iota(jnp.int32, (REQ, HD), 1)
     row8 = lax.broadcasted_iota(jnp.int32, (REQ, HD), 0)
@@ -182,7 +191,7 @@
     wait_all(recv_a, recv_sem.at[0])
     for head in range(HEADS):
         pair = recv_a[head].astype(jnp.float32) + recv_a[N_TP + head].astype(jnp.float32)
-        q_rot[pl.ds(head * REQ, REQ), :] = rounded(rotate(rounded(pair[:REQ])))
+        q_rot[pl.ds(head * REQ, REQ), :] = rounded(rotate(rounded(pair)))
 
     def spread(row, op):
         for shift in (4, 8, 16, 32, 64):
@@ -247,18 +256,14 @@
         w_in[:, first : first + 256 - UNITS] = jnp.zeros((HALF, 256 - UNITS), jnp.bfloat16)
     w_in[:, :UNITS] = wg[...].T
     w_in[:, 256 : 256 + UNITS] = wu[...].T
-    kv_first = (t // 8) * 8
+    wait_all(recv_kv, recv_sem.at[6], KV_PEERS)
     new_key = jnp.zeros((REQ, HD), jnp.float32)
     new_value = jnp.zeros((REQ, HD), jnp.float32)
     for j in range(4):
-        part = recv_a[kv_first + j].astype(jnp.float32) + recv_a[N_TP + kv_first + j].astype(
-            jnp.float32
-        )
-        new_key = new_key + part[REQ:]
-        part = recv_a[kv_first + 4 + j].astype(jnp.float32) + recv_a[
-            N_TP + kv_first + 4 + j
-        ].astype(jnp.float32)
-        new_value = new_value + part[REQ:]
+        new_key = new_key + (recv_kv[j].astype(jnp.float32) + recv_kv[8 + j].astype(jnp.float32))
+        new_value = new_value + (
+            recv_kv[4 + j].astype(jnp.float32) + recv_kv[12 + j].astype(jnp.float32)
+        )
     key_rot = rounded(rotate(rounded(new_key)))
     new_value = rounded(new_value)
     my_query = q_rot[pl.ds(pl.multiple_of(t * REQ, REQ), REQ), :]
@@ -344,6 +349,7 @@
     out_ref[...] = jnp.concatenate((result[:, :64], result[:, 64:]), axis=0).astype(out_ref.dtype)
 
     wait_all(recv_a, send_sem.at[0])
+    wait_all(recv_kv, send_sem.at[6], KV_PEERS)
     wait_all(recv_c, send_sem.at[1])
     wait_all(recv_d, send_sem.at[2])
     wait_all(recv_e, send_sem.at[3])
@@ -378,8 +384,9 @@
             pltpu.VMEM((REQ, 4 * CTX_DEV, HD), bf16),
             pltpu.VMEM((REQ, HD, 4 * CTX_DEV), bf16),
             pltpu.VMEM((REQ, 4 * CTX_DEV, HD), bf16),
-            pltpu.VMEM((16, HD), bf16),
-            pltpu.VMEM((PEERS, 16, HD), bf16),
+            pltpu.VMEM((2, REQ, HD), bf16),
+            pltpu.VMEM((PEERS, REQ, HD), bf16),
+            pltpu.VMEM((KV_PEERS, REQ, HD), bf16),
             pltpu.VMEM((HEADS * REQ, HD), f32),
             pltpu.VMEM((HEADS * 16, HD), f32),
             pltpu.VMEM((HEADS, 16, HD), bf16),
@@ -394,8 +401,8 @@
             pltpu.VMEM((REQ, HALF), bf16),
             pltpu.SemaphoreType.DMA((12,)),
             pltpu.SemaphoreType.DMA((2 * REQ,)),
-            pltpu.SemaphoreType.DMA((6,)),
-            pltpu.SemaphoreType.DMA((6,)),
+            pltpu.SemaphoreType.DMA((7,)),
+            pltpu.SemaphoreType.DMA((7,)),
         ],
         compiler_params=pltpu.CompilerParams(
             collective_id=0, has_side_effects=True, vmem_limit_bytes=60 << 20

time: 51.7 us -> 50.8 us (0.983)
  Pallas kernels: 50.3 us -> 49.4 us
    pallas_call x1, Pallas kernels: 50.3 us -> 49.4 us  [on_device(): pl.pallas_call(layer, out_shape=jax.ShapeDtypeStruct((REQ, 64), bf16), in...]
where the time goes in v3:
time: 50.8 us; the launch traced here: 50.7 us
  Pallas kernels  49.4 us (97%)
  local copies, waits for them, and re-layouts  1.26 us (2%)
    pallas_call x1, Pallas kernels, on_device(): pl.pallas_call(layer, out_shape=jax.ShapeDtypeStruct((REQ, 64), bf16), in...  49.4 us
    unnamed x1, local copies, waits for them, and re-layouts  1.26 us

profile of v3, /device:TPU:1, one launch (start us, length us, event | category | flops | bytes accessed | tf_op | source)
XLA Modules:
  0.0 50.7 jit_solution(10185573107690594637)
XLA Ops:
  0.0 49.4 %shard_map.118 = bf16[8,64]{1,0:T(8,128)(2,1)} custom-call(bf16[8,8192]{1,0:T(8,128)(2,1)} %hidden_ref.1, f32[1,8192]{1,0:T(1,128)} %bitcast.14, f32[1,8192]{1,0:T(1,128)} %bitcast.15, bf16[4096,128]{1,0:T(8,128)(2,1)} %bitcast.11, bf16[32,4096]{1,0:T(8,128)(2,1)} %bitcast.13, bf16[128,4096]{1,0:T(8,128)(2,1)} %bitcast.12, bf16[224,4096]{1,0:T(8,128)(2,1)} %bitcast.9, ...), custom_call_target="tpu_custom_call" | custom-call | tf_op jit(solution)/shard_map/pallas_call | solution.py:366
  49.4 1.3 %copy.14 = bf16[8,64]{1,0:T(8,128)(2,1)} copy(bf16[8,64]{1,0:T(8,128)(2,1)} %shard_map.118) | data formatting | bytes 2048

commit v4 on v3

--- a/solution.py
+++ b/solution.py
@@ -57,18 +57,19 @@
         return 2 + i - (i // 2) * (2 * i - 1)
 
     def row_peer(k):
-        there = (me_row + 1 + k) % PEERS
-        return there, (there // N_TP, there % N_TP, r)
-
+        there = lax.rem(me_row + 1 + k, PEERS)
+        return there, (lax.div(there, N_TP), lax.rem(there, N_TP), r)
+
+    kv_first = (t // 8) * 8
     me_kv = g * 8 + t % 8
 
     def kv_peer(k):
-        there = (me_kv + 1 + k) % KV_PEERS
-        return there, (there // 8, (t // 8) * 8 + there % 8, r)
+        there = lax.rem(me_kv + 1 + k, KV_PEERS)
+        return there, (lax.div(there, 8), kv_first + lax.rem(there, 8), r)
 
     def col_peer(k):
-        there = (me_col + 1 + k) % PEERS
-        return there, (g, there // 2, there % 2)
+        there = lax.rem(me_col + 1 + k, PEERS)
+        return there, (g, lax.div(there, 2), lax.rem(there, 2))
 
     barrier = pltpu.get_barrier_semaphore()
 
@@ -136,7 +137,7 @@
     pl.semaphore_wait(barrier, PEERS)
 
     def send_all(peer, source, landing, stage, peers=PEERS):
-        @pl.loop(0, peers - 1)
+        @pl.loop(0, peers - 1, unroll=9 if peers == PEERS else 1)
         def _(k):
             p, dev = peer(k)
             pltpu.make_async_remote_copy(
@@ -248,7 +249,7 @@
     for head in range(HEADS):
         send_c[head] = stage_c[pl.ds(head * 16, 16), :].astype(jnp.bfloat16)
     recv_c[me_row] = send_c[t]
-    send_all(row_peer, lambda p: send_c.at[p % N_TP], recv_c.at[me_row], 1)
+    send_all(row_peer, lambda p: send_c.at[lax.rem(p, N_TP)], recv_c.at[me_row], 1)
 
     for c in copies[7:9]:
         c.wait()

time: 50.8 us -> 49.1 us (0.967)
  Pallas kernels: 49.4 us -> 47.6 us
    pallas_call x1, Pallas kernels: 49.4 us -> 47.6 us  [on_device(): pl.pallas_call(layer, out_shape=jax.ShapeDtypeStruct((REQ, 64), bf16), in...]
where the time goes in v4:
time: 49.1 us; the launch traced here: 48.9 us
  Pallas kernels  47.6 us (97%)
  local copies, waits for them, and re-layouts  1.26 us (3%)
    pallas_call x1, Pallas kernels, on_device(): pl.pallas_call(layer, out_shape=jax.ShapeDtypeStruct((REQ, 64), bf16), in...  47.6 us
    unnamed x1, local copies, waits for them, and re-layouts  1.26 us

profile of v4, /device:TPU:1, one launch (start us, length us, event | category | flops | bytes accessed | tf_op | source)
XLA Modules:
  0.0 48.9 jit_solution(15967201747868556081)
XLA Ops:
  0.0 47.6 %shard_map.118 = bf16[8,64]{1,0:T(8,128)(2,1)} custom-call(bf16[8,8192]{1,0:T(8,128)(2,1)} %hidden_ref.1, f32[1,8192]{1,0:T(1,128)} %bitcast.14, f32[1,8192]{1,0:T(1,128)} %bitcast.15, bf16[4096,128]{1,0:T(8,128)(2,1)} %bitcast.11, bf16[32,4096]{1,0:T(8,128)(2,1)} %bitcast.13, bf16[128,4096]{1,0:T(8,128)(2,1)} %bitcast.12, bf16[224,4096]{1,0:T(8,128)(2,1)} %bitcast.9, ...), custom_call_target="tpu_custom_call" | custom-call | tf_op jit(solution)/shard_map/pallas_call | solution.py:367
  47.6 1.3 %copy.14 = bf16[8,64]{1,0:T(8,128)(2,1)} copy(bf16[8,64]{1,0:T(8,128)(2,1)} %shard_map.118) | data formatting | bytes 2048

commit v5 on v2

--- a/solution.py
+++ b/solution.py
@@ -56,16 +56,16 @@
         return 2 + i - (i // 2) * (2 * i - 1)
 
     def row_peer(k):
-        there = (me_row + 1 + k) % PEERS
-        return there, (there // N_TP, there % N_TP, r)
+        there = lax.rem(me_row + 1 + k, PEERS)
+        return there, (lax.div(there, N_TP), lax.rem(there, N_TP), r)
 
     def col_peer(k):
-        there = (me_col + 1 + k) % PEERS
-        return there, (g, there // 2, there % 2)
+        there = lax.rem(me_col + 1 + k, PEERS)
+        return there, (g, lax.div(there, 2), lax.rem(there, 2))
 
     barrier = pltpu.get_barrier_semaphore()
 
-    @pl.loop(0, PEERS - 1)
+    @pl.loop(0, PEERS - 1, unroll=9)
     def _(k):
         _, dev = row_peer(k)
         pl.semaphore_signal(barrier, inc=1, device_id=dev, device_id_type=MESH)
@@ -128,7 +128,7 @@
     pl.semaphore_wait(barrier, PEERS)
 
     def send_all(peer, source, landing, stage):
-        @pl.loop(0, PEERS - 1)
+        @pl.loop(0, PEERS - 1, unroll=9)
         def _(k):
             p, dev = peer(k)
             pltpu.make_async_remote_copy(
@@ -239,7 +239,7 @@
     for head in range(HEADS):
         send_c[head] = stage_c[pl.ds(head * 16, 16), :].astype(jnp.bfloat16)
     recv_c[me_row] = send_c[t]
-    send_all(row_peer, lambda p: send_c.at[p % N_TP], recv_c.at[me_row], 1)
+    send_all(row_peer, lambda p: send_c.at[lax.rem(p, N_TP)], recv_c.at[me_row], 1)
 
     for c in copies[7:9]:
         c.wait()

time: 51.7 us -> 49.8 us (0.963)
  Pallas kernels: 50.3 us -> 48.4 us
    pallas_call x1, Pallas kernels: 50.3 us -> 48.4 us  [on_device(): pl.pallas_call(layer, out_shape=jax.ShapeDtypeStruct((REQ, 64), bf16), in...]
where the time goes in v5:
time: 49.8 us; the launch traced here: 49.7 us
  Pallas kernels  48.4 us (97%)
  local copies, waits for them, and re-layouts  1.26 us (3%)
    pallas_call x1, Pallas kernels, on_device(): pl.pallas_call(layer, out_shape=jax.ShapeDtypeStruct((REQ, 64), bf16), in...  48.4 us
    unnamed x1, local copies, waits for them, and re-layouts  1.26 us

profile of v5, /device:TPU:1, one launch (start us, length us, event | category | flops | bytes accessed | tf_op | source)
XLA Modules:
  0.0 49.7 jit_solution(14824082235918720006)
XLA Ops:
  0.0 48.4 %shard_map.118 = bf16[8,64]{1,0:T(8,128)(2,1)} custom-call(bf16[8,8192]{1,0:T(8,128)(2,1)} %hidden_ref.1, f32[1,8192]{1,0:T(1,128)} %bitcast.14, f32[1,8192]{1,0:T(1,128)} %bitcast.15, bf16[4096,128]{1,0:T(8,128)(2,1)} %bitcast.11, bf16[32,4096]{1,0:T(8,128)(2,1)} %bitcast.13, bf16[128,4096]{1,0:T(8,128)(2,1)} %bitcast.12, bf16[224,4096]{1,0:T(8,128)(2,1)} %bitcast.9, ...), custom_call_target="tpu_custom_call" | custom-call | tf_op jit(solution)/shard_map/pallas_call | solution.py:360
  48.4 1.3 %copy.14 = bf16[8,64]{1,0:T(8,128)(2,1)} copy(bf16[8,64]{1,0:T(8,128)(2,1)} %shard_map.118) | data formatting | bytes 2048
